TPU v7x, 512 devices: a whole 4x4x16 slice. The times are simulated.
512 devices in a mesh: sample: 32 (over z_lo, y), tok: 16 (over z_hi, x, core).
Axes of the slice: x: 4, y: 4, z: 16 (z_hi: 2, z_lo: 8; z = z_hi * 8 + z_lo), core: 2. Of those that a mesh axis runs over, the one named last changes fastest.
Arguments:
- noisy_tokens: bfloat16 [32, 512, 768], P('sample', 'tok'), may hold values from -6 to 6
- pair_bias: bfloat16 [16, 512, 512], P(None, 'tok', 'sample'), may hold values from -3 to 305
- chain_ids: int32 [512], replicated, may hold values from 0 to 7, never falling along the last dimension, each value on 1 to 128 neighbouring positions
- pad_mask: int32 [512], replicated, may hold values 0 or 1
- step_index: int32 [32], P('sample'), may hold values from 0 to 199
- chain_gain: float32 [16], replicated, may hold values from -3 to 3
- w_query: bfloat16 [768, 768], replicated, may hold values from -0.21875 to 0.21875
- w_key: bfloat16 [768, 768], replicated, may hold values from -0.21875 to 0.21875
- w_value: bfloat16 [768, 768], replicated, may hold values from -0.21875 to 0.21875
- w_output: bfloat16 [768, 768], replicated, may hold values from -0.21875 to 0.21875
Outputs:
- denoised: bfloat16 [32, 512, 768], P('sample', 'tok')
Inputs may be any that keep to these rules, and one draw needn't show every extreme that they name: `chain_ids`: chains are contiguous runs of 1 to 128 tokens, numbered in order.
All inputs are finite; a program needn't handle non-finite values.
Results may differ from a plain program's by a relative error of at most 0.0034.
Values may be sent and summed in bfloat16 or wider, within the bound.
A program may use at most 64 MiB of HBM per device.

v0:
```python
import math
import jax
import jax.numpy as jnp
from jax import lax
from jax.sharding import PartitionSpec as P

STEPS = 200
sigma_data = 16.0
sigma_top = 160.0
sigma_low = 0.0004
rho_exp = 7.0


def layer_norm(values):
    xf = values.astype(jnp.float32)
    center = xf - jnp.mean(xf, axis=-1, keepdims=True)
    spread = jnp.mean(center * center, axis=-1, keepdims=True)
    return (center * lax.rsqrt(spread + 1e-05)).astype(jnp.bfloat16)


def noise_factors(step_index):
    ratio = step_index.astype(jnp.float32) / (STEPS - 1)
    upper = sigma_top ** (1.0 / rho_exp)
    lower = sigma_low ** (1.0 / rho_exp)
    sigma = sigma_data * (upper + ratio * (lower - upper)) ** rho_exp
    skip_scale = sigma_data**2 / (sigma_data**2 + sigma * sigma)
    out_scale = sigma / jnp.sqrt(sigma * sigma + sigma_data**2)
    return (skip_scale, out_scale)


def project(flat, weight):
    return jnp.dot(flat, weight, preferred_element_type=jnp.float32).astype(jnp.bfloat16)


def shards(
    noisy_tokens,
    pair_bias,
    chain_ids,
    pad_mask,
    step_index,
    chain_gain,
    w_query,
    w_key,
    w_value,
    w_output,
):
    samples, rows, width = noisy_tokens.shape
    heads = chain_gain.shape[0]
    head_size = width // heads
    start = lax.axis_index("tok") * rows
    chain_rows = lax.dynamic_slice_in_dim(chain_ids, start, rows)
    normed = layer_norm(noisy_tokens)
    flat = normed.reshape(samples * rows, width)
    queries = project(flat, w_query).reshape(samples, rows, heads, head_size)
    bias_rows = lax.all_gather(pair_bias, "sample", axis=2, tiled=True)
    everyone = lax.all_gather(normed, "tok", axis=1, tiled=True)
    total = everyone.shape[1]
    every_flat = everyone.reshape(samples * total, width)
    key_rows = project(every_flat, w_key).reshape(samples, total, heads, head_size)
    value_rows = project(every_flat, w_value).reshape(samples, total, heads, head_size)
    same_chain = (chain_rows[:, None] == chain_ids[None, :]).astype(jnp.float32)
    masked = (pad_mask.astype(jnp.float32) - 1.0) * 1000000000.0
    scale_root = jnp.sqrt(jnp.float32(head_size))
    group = math.gcd(heads, 4)
    pieces = []
    for first in range(0, heads, group):
        query_part = queries[:, :, first : first + group]
        key_part = key_rows[:, :, first : first + group]
        value_part = value_rows[:, :, first : first + group]
        scores = jnp.einsum(
            "sihd,sjhd->shij", query_part, key_part, preferred_element_type=jnp.float32
        )
        scores = scores / scale_root
        scores = scores + bias_rows[first : first + group].astype(jnp.float32)[None]
        gains = chain_gain[first : first + group]
        scores = (
            scores
            + gains[None, :, None, None] * same_chain[None, None]
            + masked[None, None, None, :]
        )
        top = jnp.max(scores, axis=-1, keepdims=True)
        expo = jnp.exp(scores - top)
        weights = (expo / jnp.sum(expo, axis=-1, keepdims=True)).astype(jnp.bfloat16)
        attended_part = jnp.einsum(
            "shij,sjhd->sihd", weights, value_part, preferred_element_type=jnp.float32
        )
        pieces.append(attended_part.astype(jnp.bfloat16))
    attended = jnp.concatenate(pieces, axis=2).reshape(samples * rows, width)
    projected = jnp.dot(attended, w_output, preferred_element_type=jnp.float32).reshape(
        samples, rows, width
    )
    skip_scale, out_scale = noise_factors(step_index)
    mixed = (
        skip_scale[:, None, None] * noisy_tokens.astype(jnp.float32)
        + out_scale[:, None, None] * projected
    )
    return mixed.astype(jnp.bfloat16)


def solution(mesh):
    in_specs = (
        P("sample", "tok", None),
        P(None, "tok", "sample"),
        P(),
        P(),
        P("sample"),
        P(),
        P(),
        P(),
        P(),
        P(),
    )
    out_specs = P("sample", "tok", None)
    return jax.shard_map(shards, mesh=mesh, in_specs=in_specs, out_specs=out_specs, check_vma=False)
```

profile of v0, /device:TPU:8, one launch (start us, length us, event | category | flops | bytes accessed | tf_op | source)
XLA Modules:
  0.0 214.3 jit_solution(18400831928374968863)
XLA Ops:
  0.0 0.0 copy-start
  0.0 1.0 convert_reduce_fusion
  1.0 1.0 fusion.39
  2.0 0.9 fusion.40
  2.9 0.0 copy-start.6
  2.9 0.6 copy-done.6
  3.5 55.3 %all_gather.6 = bf16[1,512,768]{2,1,0:T(8,128)(2,1)S(1)} all-gather(bf16[1,32,768]{2,1,0:T(8,128)(2,1)S(1)} %fusion.40), channel_id=1, replica_groups=mesh['sample'=32,'tok'=16] {'tok'}, dimensions={1}, use_global_device_ids=true | all-gather | bytes 835584 | tf_op jit(solution)/shard_map/all_gather | solution.py:56
  58.8 0.0 copy-start.5
  58.8 0.9 copy-done.5
  59.7 0.0 copy-done
  59.7 0.8 convolution_convert_fusion.1
  60.5 0.0 copy-start.9
  60.5 1.2 copy.32
  61.7 0.0 copy-done.9
  61.7 123.6 %all_gather.7 = bf16[16,32,512]{1,0,2:T(8,128)(2,1)S(1)} all-gather(bf16[16,32,16]{1,0,2:T(8,128)(2,1)S(1)} %copy.35), channel_id=1, replica_groups=mesh['sample'=32,'tok'=16] {'sample'}, dimensions={2}, use_global_device_ids=true | all-gather | bytes 540672 | tf_op jit(solution)/shard_map/all_gather | solution.py:55
  185.2 0.8 fusion.46
  186.1 0.9 copy.51
  187.0 3.2 %convolution_convert_fusion = bf16[512,768]{1,0:T(8,128)(2,1)} fusion(bf16[768,768]{1,0:T(8,128)(2,1)} %param.17, bf16[1,512,768]{2,1,0:T(8,128)(2,1)} %copy-done.5), kind=kOutput, calls=%fused_computation.4 | convolution fusion | flops 604372992 | bytes 2752512 | tf_op jit(solution)/shard_map/dot_general | solution.py:32
  190.2 0.0 copy-start.11
  190.2 1.4 copy.34
  191.6 0.0 copy-done.11
  191.6 0.6 fusion.48
  192.2 0.7 add_multiply_fusion
  192.9 0.8 dynamic_slice.3
  193.7 1.4 compare_convert_fusion
  195.0 2.2 %convolution_convert_fusion.2 = bf16[32,768]{1,0:T(8,128)(2,1)} fusion(bf16[768,768]{1,0:T(8,128)(2,1)} %param.16, bf16[1,32,768]{2,1,0:T(8,128)(2,1)} %copy-done.6), kind=kOutput, calls=%fused_computation.34 | convolution fusion | flops 37773312 | bytes 1277952 | tf_op jit(solution)/shard_map/dot_general | solution.py:32
  197.3 1.6 reshape.229
  198.9 1.6 fusion.47
  200.5 1.1 fusion.19
  201.6 0.0 copy-start.3
  201.6 0.7 copy-done.3
  202.3 0.2 fusion.49
  202.5 2.1 fusion.30
  204.6 0.9 copy.49
  205.5 1.1 fusion.18
  206.6 0.0 copy-start.1
  206.6 0.0 copy-start.8
  206.7 0.2 fusion.50
  206.9 1.3 fusion.29
  208.1 0.3 copy.47
  208.4 0.0 copy-done.1
  208.4 0.0 copy-done.8
  208.4 0.2 fusion.17
  208.6 0.0 copy-start.7
  208.6 0.2 fusion.51
  208.8 1.3 fusion.28
  210.1 0.3 copy.45
  210.4 0.0 copy-start.10
  210.4 0.0 copy-done.7
  210.4 0.2 fusion.16
  210.6 0.0 copy-start.2
  210.6 0.0 copy-start.4
  210.6 0.2 fusion.52
  210.8 1.4 fusion.27
  212.2 0.0 copy-done.10
  212.3 0.1 copy.43
  212.3 0.2 reshape.242
  213.3 0.0 copy-done.2
  213.3 0.0 copy-done.4
  213.3 1.0 fusion.26
  (4 shorter events, 0.1 us)
Async XLA Ops:
  0.0 59.7 %copy-start = (bf16[768,768]{1,0:T(8,128)(2,1)S(1)}, bf16[768,768]{1,0:T(8,128)(2,1)}, u32[]{:S(2)}) copy-start(bf16[768,768]{1,0:T(8,128)(2,1)} %param.18) | copy-start | bytes 3538948
  2.9 0.6 copy-start.6
  58.8 0.9 copy-start.5
  60.5 1.2 copy-start.9
  190.2 1.4 copy-start.11
  201.6 0.7 copy-start.3
  206.6 1.8 copy-start.1
  206.6 1.8 copy-start.8
  208.6 1.8 copy-start.7
  210.4 1.8 copy-start.10
  210.6 2.7 %copy-start.2 = (bf16[768,768]{1,0:T(8,128)(2,1)S(1)}, bf16[768,768]{1,0:T(8,128)(2,1)}, u32[]{:S(2)}) copy-start(bf16[768,768]{1,0:T(8,128)(2,1)} %param.19) | copy-start | bytes 3538948
  210.6 2.7 %copy-start.4 = (bf16[1,32,768]{2,1,0:T(8,128)(2,1)S(1)}, bf16[1,32,768]{2,1,0:T(8,128)(2,1)}, u32[]{:S(2)}) copy-start(bf16[1,32,768]{2,1,0:T(8,128)(2,1)} %param.10) | copy-start | bytes 147460
where the time goes:
time: 215 us; the launch traced here: 214 us
  blocking collectives  179 us (83%)
  matrix products  15.7 us (7%)
  local copies, waits for them, and re-layouts  13 us (6%)
  other arithmetic  5.78 us (3%)
    all_gather x1, blocking collectives, shards(): bias_rows = lax.all_gather(pair_bias, 'sample', axis=2, tiled=True)  124 us
    all_gather x1, blocking collectives, shards(): everyone = lax.all_gather(normed, 'tok', axis=1, tiled=True)  55.3 us
    dot_general x3, matrix products, project(): jnp.dot(flat, weight, preferred_element_type=jnp.float32)  6.2 us
    dot_general x4, matrix products, shards(): jnp.einsum('shij,sjhd->sihd', weights, value_part, preferred_element_type...  6.01 us
    unnamed x29, local copies, waits for them, and re-layouts  4.77 us

commit v1 on v0

--- a/solution.py
+++ b/solution.py
@@ -52,7 +52,9 @@
     normed = layer_norm(noisy_tokens)
     flat = normed.reshape(samples * rows, width)
     queries = project(flat, w_query).reshape(samples, rows, heads, head_size)
-    bias_rows = lax.all_gather(pair_bias, "sample", axis=2, tiled=True)
+    bias_rows = jnp.concatenate(
+        lax.all_to_all(jnp.stack([pair_bias] * lax.axis_size("sample")), "sample", 0, 0), axis=2
+    )
     everyone = lax.all_gather(normed, "tok", axis=1, tiled=True)
     total = everyone.shape[1]
     every_flat = everyone.reshape(samples * total, width)

time: 215 us -> 112 us (0.52)
  the two profiles are of different devices: /device:TPU:8 before, /device:TPU:169 now
where the time goes in v1:
time: 112 us; the launch traced here: 111 us
  blocking collectives  63.6 us (57%)
  local copies, waits for them, and re-layouts  16 us (14%)
  matrix products  14.3 us (13%)
  starting transfers between devices  13 us (12%)
  other arithmetic  3.13 us (3%)
    all_gather x1, blocking collectives, shards(): everyone = lax.all_gather(normed, 'tok', axis=1, tiled=True)  63.6 us
    all_to_all x1, starting transfers between devices, shards(): lax.all_to_all(jnp.stack([pair_bias] * lax.axis_size('sample')), 'sample'...  13 us
    unnamed x21, local copies, waits for them, and re-layouts  7.72 us
    dot_general x4, matrix products, shards(): jnp.einsum('shij,sjhd->sihd', weights, value_part, preferred_element_type...  5.4 us
    convert_element_type x8, local copies, waits for them, and re-layouts, shards(): scores = scores + bias_rows[first:first + group].astype(jnp.float32)[None]  4.95 us
    dot_general x4, matrix products, shards(): jnp.einsum('sihd,sjhd->shij', query_part, key_part, preferred_element_typ...  4.84 us
    dot_general x3, matrix products, project(): jnp.dot(flat, weight, preferred_element_type=jnp.float32)  3.14 us
    convert_element_type x2, local copies, waits for them, and re-layouts, project(): jnp.dot(flat, weight, preferred_element_type=jnp.float32)  2.35 us
  transfers between devices with their start and end apart: 1, of which 0 were waited for; matrix products, arithmetic and copies ran while one was open for 6% of the time, Pallas kernels for 0%

profile of v1, /device:TPU:169, one launch (start us, length us, event | category | flops | bytes accessed | tf_op | source)
XLA Modules:
  0.0 111.1 jit_solution(10098428244615445892)
XLA Ops:
  0.0 0.0 copy-start
  0.0 1.4 %broadcast_bitcast_fusion = bf16[32,16,16,32]{3,2,1,0:T(8,128)(2,1)S(1)} fusion(bf16[16,32,16]{1,2,0:T(8,128)(2,1)} %param.11), kind=kLoop, calls=%fused_computation.93 | loop fusion | bytes 540672
  1.4 0.0 copy-start.5
  1.4 2.7 %reshape.266 = bf16[32,2,4096]{2,1,0:T(2,128)(2,1)} reshape(bf16[32,16,16,32]{3,2,1,0:T(8,128)(2,1)S(1)} %broadcast_bitcast_fusion) | data formatting | bytes 1048576
  4.1 13.0 %all-to-all-start = ((bf16[32,2,4096]{2,1,0:T(2,128)(2,1)}), bf16[32,2,4096]{2,1,0:T(2,128)(2,1)}, u32[]{:S(2)}, u32[]{:S(2)}) async-start(bf16[32,2,4096]{2,1,0:T(2,128)(2,1)} %reshape.266), calls=%async_computation | async-start | bytes 1048576 | tf_op jit(solution)/shard_map/all_to_all | solution.py:56
  17.9 0.0 copy-done.5
  17.9 0.1 convert_reduce_fusion
  18.1 0.2 fusion.39
  18.3 0.1 fusion.40
  18.4 63.6 %all_gather.3 = bf16[1,512,768]{2,1,0:T(8,128)(2,1)S(1)} all-gather(bf16[1,32,768]{2,1,0:T(8,128)(2,1)S(1)} %fusion.40), channel_id=1, replica_groups=mesh['sample'=32,'tok'=16] {'tok'}, dimensions={1}, use_global_device_ids=true | all-gather | bytes 835584 | tf_op jit(solution)/shard_map/all_gather | solution.py:58
  81.9 0.0 copy-done
  81.9 0.8 convolution_convert_fusion.1
  82.7 1.2 %copy.35 = bf16[512,768]{0,1:T(8,128)(2,1)} copy(bf16[512,768]{1,0:T(8,128)(2,1)S(1)} %convolution_convert_fusion.1) | data formatting | bytes 1572864 | tf_op jit(solution)/shard_map/convert_element_type | solution.py:32
  83.9 2.0 %convolution_convert_fusion = bf16[512,768]{1,0:T(8,128)(2,1)S(1)} fusion(bf16[768,768]{1,0:T(8,128)(2,1)} %param.17, bf16[1,512,768]{2,1,0:T(8,128)(2,1)S(1)} %all_gather.3), kind=kOutput, calls=%fused_computation.4 | convolution fusion | flops 604372992 | bytes 2752512 | tf_op jit(solution)/shard_map/dot_general | solution.py:32
  86.0 0.0 copy-start.2
  86.0 0.0 copy-start.7
  86.0 0.0 copy-start.6
  86.0 0.0 copy-start.8
  86.0 1.2 %copy.37 = bf16[512,768]{0,1:T(8,128)(2,1)} copy(bf16[512,768]{1,0:T(8,128)(2,1)S(1)} %convolution_convert_fusion) | data formatting | bytes 1572864 | tf_op jit(solution)/shard_map/convert_element_type | solution.py:32
  87.2 0.1 copy-done.2
  87.3 0.3 convolution_convert_fusion.2
  87.6 0.2 reshape.247
  87.8 0.0 copy-done.7
  87.8 0.1 dynamic_slice.3
  87.9 0.0 copy-done.6
  87.9 0.1 fusion.47
  87.9 0.0 copy-done.8
  88.0 0.1 compare_convert_fusion
  88.0 0.1 fusion.46
  88.1 0.0 all-to-all-done
  88.1 3.0 %reshape.267 = bf16[32,16,16,32]{3,2,1,0:T(8,128)(2,1)S(1)} reshape(bf16[32,2,4096]{2,1,0:T(2,128)(2,1)} %all-to-all-done) | data formatting | bytes 1048576
  91.1 0.4 bitcast_bitcast_fusion
  91.5 1.8 %slice_convert_fusion.3 = (f32[4,32,32,16]{1,3,0,2:T(8,128)S(1)}, f32[4,32,32,16]{1,3,0,2:T(8,128)S(1)}, f32[4,32,32,16]{1,3,0,2:T(8,128)}, f32[4,32,32,16]{1,3,0,2:T(8,128)}) fusion(bf16[16,32,32,16]{1,3,0,2:T(8,128)(2,1)S(1)} %bitcast_bitcast_fusion), kind=kLoop, calls=%fused_computation.48 | loop fusion | flops 262144 | bytes 1572864 | tf_op jit(solution)/shard_map/convert_element_type | solution.py:76
  93.3 0.1 copy.47
  93.4 1.0 copy.48
  94.4 0.0 copy-start.1
  94.4 1.3 %fusion.19 = f32[4,32,512]{2,1,0:T(8,128)S(1)} fusion(f32[4,32,512]{2,1,0:T(8,128)} %copy.48, bf16[1,512,16,48]{1,3,2,0:T(8,128)(2,1)} %bitcast.99, f32[4]{0:T(128)S(1)} %get-tuple-element.15, f32[512]{0:T(512)S(1)} %add_multiply_fusion, f32[32,512]{1,0:T(8,128)S(1)} %compare_convert_fusion, bf16[1,32,4,48]{3,2,1,0:T(4,128)(2,1)S(1)} %get-tuple-element.12), kind=kOutput, calls=%fused_computation.25 | convolution fusion | flops 6619136 | bytes 800784 | tf_op jit(solution)/shard_map/sihd,sjhd->shij/dot_general | solution.py:72
  95.7 0.0 copy-start.4
  95.7 0.2 fusion.48
  95.9 0.5 copy-done.4
  96.4 0.0 copy-done.1
  96.4 0.1 copy.44
  96.5 1.0 copy.45
  97.5 1.2 %fusion.18 = f32[4,32,512]{2,1,0:T(8,128)S(1)} fusion(f32[4,32,512]{2,1,0:T(8,128)} %copy.45, bf16[1,512,16,48]{1,3,2,0:T(8,128)(2,1)} %bitcast.100, f32[4]{0:T(128)S(1)} %get-tuple-element.16, f32[512]{0:T(512)S(1)} %add_multiply_fusion, f32[32,512]{1,0:T(8,128)S(1)} %compare_convert_fusion, bf16[1,32,4,48]{3,2,1,0:T(4,128)(2,1)S(1)} %get-tuple-element.10), kind=kOutput, calls=%fused_computation.24 | convolution fusion | flops 6619136 | bytes 800784 | tf_op jit(solution)/shard_map/sihd,sjhd->shij/dot_general | solution.py:72
  98.7 0.2 fusion.49
  98.9 1.5 %fusion.30 = bf16[1,32,4,48]{3,1,2,0:T(8,128)(2,1)S(1)} fusion(bf16[1,512,16,48]{1,3,2,0:T(8,128)(2,1)} %bitcast.103, f32[4,32]{1,0:T(4,128)S(1)} %fusion.48, f32[4,32,512]{2,1,0:T(8,128)} %copy-done.4), kind=kOutput, calls=%fused_computation.42 | convolution fusion | flops 6494847 | bytes 733696 | tf_op jit(solution)/shard_map/shij,sjhd->sihd/dot_general | solution.py:86
  100.4 1.3 %fusion.29 = bf16[1,32,4,48]{3,1,2,0:T(8,128)(2,1)S(1)} fusion(bf16[1,512,16,48]{1,3,2,0:T(8,128)(2,1)} %bitcast.104, f32[4,32]{1,0:T(4,128)S(1)} %fusion.49, f32[4,32,512]{2,1,0:T(8,128)S(1)} %fusion.18), kind=kOutput, calls=%fused_computation.41 | convolution fusion | flops 6494847 | bytes 735232 | tf_op jit(solution)/shard_map/shij,sjhd->sihd/dot_general | solution.py:86
  101.7 1.3 %copy.41 = f32[4,32,32,16]{1,3,2,0:T(8,128)S(1)} copy(f32[4,32,32,16]{1,3,0,2:T(8,128)} %get-tuple-element.8) | data formatting | bytes 524288 | tf_op jit(solution)/shard_map/convert_element_type | solution.py:76
  103.0 1.0 copy.42
  104.0 1.2 %fusion.17 = f32[4,32,512]{2,1,0:T(8,128)S(1)} fusion(f32[4,32,512]{2,1,0:T(8,128)} %copy.42, bf16[1,512,16,48]{1,3,2,0:T(8,128)(2,1)} %bitcast.101, f32[4]{0:T(128)S(1)} %get-tuple-element.14, f32[512]{0:T(512)S(1)} %add_multiply_fusion, f32[32,512]{1,0:T(8,128)S(1)} %compare_convert_fusion, bf16[1,32,4,48]{3,2,1,0:T(4,128)(2,1)S(1)} %get-tuple-element.11), kind=kOutput, calls=%fused_computation.23 | convolution fusion | flops 6619136 | bytes 800784 | tf_op jit(solution)/shard_map/sihd,sjhd->shij/dot_general | solution.py:72
  105.3 0.2 fusion.50
  105.5 1.3 %fusion.28 = bf16[1,32,4,48]{3,1,2,0:T(8,128)(2,1)S(1)} fusion(bf16[1,512,16,48]{1,3,2,0:T(8,128)(2,1)} %bitcast.105, f32[4,32]{1,0:T(4,128)S(1)} %fusion.50, f32[4,32,512]{2,1,0:T(8,128)S(1)} %fusion.17), kind=kOutput, calls=%fused_computation.40 | convolution fusion | flops 6494847 | bytes 735232 | tf_op jit(solution)/shard_map/shij,sjhd->sihd/dot_general | solution.py:86
  106.7 0.1 copy.38
  106.8 0.3 copy.39
  107.1 1.1 fusion.16
  108.2 0.0 copy-start.3
  108.3 0.2 fusion.51
  108.5 1.4 %fusion.27 = bf16[1,32,4,48]{3,1,2,0:T(8,128)(2,1)S(1)} fusion(bf16[1,512,16,48]{1,3,2,0:T(8,128)(2,1)} %bitcast.106, f32[4,32]{1,0:T(4,128)S(1)} %fusion.51, f32[4,32,512]{2,1,0:T(8,128)S(1)} %fusion.16), kind=kOutput, calls=%fused_computation.39 | convolution fusion | flops 6494847 | bytes 735232 | tf_op jit(solution)/shard_map/shij,sjhd->sihd/dot_general | solution.py:86
  109.9 0.1 copy.49
  109.9 0.2 reshape.261
  110.1 0.0 copy-done.3
  110.1 1.0 fusion.26
  (4 shorter events, 0.1 us)
Async XLA Ops:
  0.0 81.9 %copy-start = (bf16[768,768]{1,0:T(8,128)(2,1)S(1)}, bf16[768,768]{1,0:T(8,128)(2,1)}, u32[]{:S(2)}) copy-start(bf16[768,768]{1,0:T(8,128)(2,1)} %param.18) | copy-start | bytes 3538948
  1.4 16.5 %copy-start.5 = (bf16[1,32,768]{2,1,0:T(8,128)(2,1)S(1)}, bf16[1,32,768]{2,1,0:T(8,128)(2,1)}, u32[]{:S(2)}) copy-start(bf16[1,32,768]{2,1,0:T(8,128)(2,1)} %param.10) | copy-start | bytes 147460
  4.1 84.0 %all-to-all-start = ((bf16[32,2,4096]{2,1,0:T(2,128)(2,1)}), bf16[32,2,4096]{2,1,0:T(2,128)(2,1)}, u32[]{:S(2)}, u32[]{:S(2)}) async-start(bf16[32,2,4096]{2,1,0:T(2,128)(2,1)} %reshape.266), calls=%async_computation | async-start | bytes 1048576 | tf_op jit(solution)/shard_map/all_to_all | solution.py:56
  86.0 1.3 %copy-start.2 = (bf16[768,768]{1,0:T(8,128)(2,1)S(1)}, bf16[768,768]{1,0:T(8,128)(2,1)}, u32[]{:S(2)}) copy-start(bf16[768,768]{1,0:T(8,128)(2,1)} %param.16) | copy-start | bytes 3538948
  86.0 1.8 %copy-start.7 = (s32[512]{0:T(512)S(1)}, s32[512]{0:T(512)}, u32[]{:S(2)}) copy-start(s32[512]{0:T(512)} %param.12) | copy-start | bytes 6148
  86.0 1.9 %copy-start.6 = (f32[16]{0:T(128)S(1)}, f32[16]{0:T(128)}, u32[]{:S(2)}) copy-start(f32[16]{0:T(128)} %param.15) | copy-start | bytes 196
  86.0 1.9 %copy-start.8 = (s32[512]{0:T(512)S(1)}, s32[512]{0:T(512)}, u32[]{:S(2)}) copy-start(s32[512]{0:T(512)} %param.13) | copy-start | bytes 6148
  94.4 2.0 %copy-start.1 = (f32[4,32,32,16]{1,3,0,2:T(8,128)S(1)}, f32[4,32,32,16]{1,3,0,2:T(8,128)}, u32[]{:S(2)}) copy-start(f32[4,32,32,16]{1,3,0,2:T(8,128)} %get-tuple-element.7) | copy-start | bytes 786436
  95.7 0.7 copy-start.4
  108.2 1.9 %copy-start.3 = (bf16[768,768]{1,0:T(8,128)(2,1)S(1)}, bf16[768,768]{1,0:T(8,128)(2,1)}, u32[]{:S(2)}) copy-start(bf16[768,768]{1,0:T(8,128)(2,1)} %param.19) | copy-start | bytes 3538948
